TPU v7x, 256 devices: a whole 4x4x8 slice. The times are simulated.
256 devices in a mesh: tm: 8 (over x, y_lo), height: 32 (over z, y_hi, core).
Axes of the slice: x: 4, y: 4 (y_hi: 2, y_lo: 2; y = y_hi * 2 + y_lo), z: 8, core: 2. Of those that a mesh axis runs over, the one named last changes fastest.
Arguments:
- latent: bfloat16 [8, 64, 104, 1536], P('tm', 'height'), may hold values from -6 to 6
- modulation: float32 [3, 1536], replicated, may hold values from -3 to 3
- cross_norm: float32 [2, 1536], replicated, may hold values from -1.5 to 1.5
- norm_gains: float32 [4, 768], replicated, may hold values from 0.5 to 8
- w_main: bfloat16 [1536, 4608], P('height'), may hold values from -0.14505926 to 0.14505926
- text_states: bfloat16 [512, 1536], replicated, may hold values from -6 to 6
- w_text: bfloat16 [1536, 1536], P(None, 'height'), may hold values from -0.10257238 to 0.10257238
- tile_offsets: int32 [3, 8, 32, 4, 8], P(None, 'tm', 'height'), may hold values from -1 to 1, as said below
- text_mask: int32 [512], replicated, may hold values from 0 to 1
Outputs:
- block_out: bfloat16 [8, 64, 104, 1536], P('tm', 'height')
Inputs may be any that keep to these rules, and one draw needn't show every extreme that they name: `tile_offsets`: for each query tile the 8 offsets are distinct and none is (0, 0, 0).
All inputs are finite; a program needn't handle non-finite values.
Results may differ from a plain program's by a relative error of at most 0.0065.
Values may be sent and summed in bfloat16 or wider, within the bound.
A program may use at most 128 MiB of HBM per device.

v0:
```python
import jax
import jax.numpy as jnp
from jax import lax
from jax.sharding import PartitionSpec as P

HD = 128
HEADS = 6
TH = 2
TW = 26


def padded(value, sides, width):
    for axis, dim in sides:
        devices, length = (lax.axis_size(axis), value.shape[dim])
        up = [(i, (i + 1) % devices) for i in range(devices - 1)]
        down = [(j, i) for i, j in up]
        last = lax.slice_in_dim(value, length - width, length, axis=dim)
        first = lax.slice_in_dim(value, 0, width, axis=dim)
        before = lax.ppermute(last, axis, up)
        after = lax.ppermute(first, axis, down)
        value = jnp.concatenate([before, value, after], axis=dim)
    return value


def layer_norm(values):
    average = jnp.mean(values, axis=-1, keepdims=True)
    centred = values - average
    variance = jnp.mean(centred * centred, axis=-1, keepdims=True)
    return centred * lax.rsqrt(variance + 1e-06)


def rms_norm(values, gain_vec):
    mean_square = jnp.mean(values * values, axis=-1, keepdims=True)
    return values * lax.rsqrt(mean_square + 1e-06) * gain_vec


def to_tiles(field_in, tile_height, tile_width):
    frame_count, row_count, col_count, channels = field_in.shape
    shaped = field_in.reshape(
        frame_count,
        row_count // tile_height,
        tile_height,
        col_count // tile_width,
        tile_width,
        channels,
    )
    shaped = shaped.transpose(0, 1, 3, 2, 4, 5)
    return shaped.reshape(
        frame_count,
        row_count // tile_height,
        col_count // tile_width,
        tile_height * tile_width,
        channels,
    )


def from_tiles(tile_set, tile_height, tile_width):
    tile_rows, tile_cols, cell_count, channels = tile_set.shape
    shaped = tile_set.reshape(tile_rows, tile_cols, tile_height, tile_width, channels)
    shaped = shaped.transpose(0, 2, 1, 3, 4)
    return shaped.reshape(tile_rows * tile_height * tile_cols * tile_width, channels)


def neighbour_index(offsets, row_base, frame_at, frame_total, row_total, tile_rows, tile_cols):
    own_step = jnp.zeros((3, tile_rows, tile_cols, 1), jnp.int32)
    step_set = jnp.concatenate([own_step, offsets], axis=3)
    frame_step = step_set[0]
    row_step = step_set[1]
    col_step = step_set[2]
    row_ids = lax.broadcasted_iota(jnp.int32, (tile_rows, tile_cols, 1), 0)
    col_ids = lax.broadcasted_iota(jnp.int32, (tile_rows, tile_cols, 1), 1)
    frame_to = frame_at + frame_step
    row_to = row_base + row_ids + row_step
    col_to = col_ids + col_step
    usable = (frame_to >= 0) & (frame_to < frame_total) & (row_to >= 0) & (row_to < row_total)
    usable = usable & (col_to >= 0) & (col_to < tile_cols)
    position = ((1 + frame_step) * (tile_rows + 2) + row_ids + 1 + row_step) * tile_cols + jnp.clip(
        col_to, 0, tile_cols - 1
    )
    return (position.reshape(-1), usable.reshape(tile_rows * tile_cols, -1))


def tile_attention(
    query_tiles, key_ext, value_ext, offsets, row_base, frame_at, frame_total, row_total
):
    tile_rows, tile_cols, cell_count, head_width = query_tiles.shape
    head_channels = head_width // HEADS
    tile_count = tile_rows * tile_cols
    position, usable = neighbour_index(
        offsets, row_base, frame_at, frame_total, row_total, tile_rows, tile_cols
    )
    key_matrix = jnp.take(key_ext.reshape(-1, cell_count, head_width), position, axis=0).reshape(
        tile_count, -1, HEADS, head_channels
    )
    value_matrix = jnp.take(
        value_ext.reshape(-1, cell_count, head_width), position, axis=0
    ).reshape(tile_count, -1, HEADS, head_channels)
    query_matrix = query_tiles.reshape(tile_count, cell_count, HEADS, head_channels)
    key_mask = jnp.repeat(usable, cell_count, axis=1)
    logit_scores = jnp.einsum(
        "tphd,tkhd->thpk", query_matrix, key_matrix, preferred_element_type=jnp.float32
    ) * head_channels ** (-0.5)
    logit_scores = jnp.where(key_mask[:, None, None, :], logit_scores, -jnp.inf)
    largest = jnp.max(logit_scores, axis=-1, keepdims=True)
    exponent = jnp.exp(logit_scores - largest)
    attention_probs = (exponent / jnp.sum(exponent, axis=-1, keepdims=True)).astype(jnp.bfloat16)
    blended_output = jnp.einsum(
        "thpk,tkhd->tphd", attention_probs, value_matrix, preferred_element_type=jnp.float32
    )
    return blended_output.astype(jnp.bfloat16).reshape(tile_rows, tile_cols, cell_count, head_width)


def cross_attention(query_flat, text_key_set, text_value_set, text_mask):
    token_count, head_width = query_flat.shape
    head_channels = head_width // HEADS
    query_matrix = query_flat.reshape(token_count, HEADS, head_channels)
    key_matrix = text_key_set.reshape(-1, HEADS, head_channels)
    logit_scores = jnp.einsum(
        "jcb,ycb->cjy", query_matrix, key_matrix, preferred_element_type=jnp.float32
    ) * head_channels ** (-0.5)
    logit_scores = jnp.where((text_mask == 1)[None, None, :], logit_scores, -jnp.inf)
    largest = jnp.max(logit_scores, axis=-1, keepdims=True)
    exponent = jnp.exp(logit_scores - largest)
    attention_probs = (exponent / jnp.sum(exponent, axis=-1, keepdims=True)).astype(jnp.bfloat16)
    value_matrix = text_value_set.reshape(-1, HEADS, head_channels)
    blended_output = jnp.einsum(
        "tgp,ptr->gtr", attention_probs, value_matrix, preferred_element_type=jnp.float32
    )
    return blended_output.astype(jnp.bfloat16).reshape(token_count, head_width)


def body(
    latent, modulation, cross_norm, norm_gains, w_main, text_states, w_text, tile_offsets, text_mask
):
    frame_count, row_count, col_count, model_dim = latent.shape
    head_width = HEADS * HD
    text_cols = lax.all_gather(w_text, "height", axis=1, tiled=True)
    text_raw = jnp.dot(text_states, text_cols, preferred_element_type=jnp.float32).astype(
        jnp.bfloat16
    )
    text_key_set = rms_norm(text_raw[:, :head_width].astype(jnp.float32), norm_gains[3]).astype(
        jnp.bfloat16
    )
    text_value_set = text_raw[:, head_width:]
    w_full = lax.all_gather(w_main, "height", axis=0, tiled=True)
    flattened = latent.reshape(-1, model_dim).astype(jnp.float32)
    modulated = (layer_norm(flattened) * (1.0 + modulation[1]) + modulation[0]).astype(jnp.bfloat16)
    joined = jnp.dot(modulated, w_full[:, : 3 * head_width], preferred_element_type=jnp.float32)
    query_out = rms_norm(joined[:, :head_width], norm_gains[0]).astype(jnp.bfloat16)
    key_out = rms_norm(joined[:, head_width : 2 * head_width], norm_gains[1]).astype(jnp.bfloat16)
    value_out = joined[:, 2 * head_width :].astype(jnp.bfloat16)
    grid_shape = (frame_count, row_count, col_count, head_width)
    stacked = jnp.stack([key_out.reshape(grid_shape), value_out.reshape(grid_shape)])
    with_rows = padded(stacked, (("height", 2),), TH)
    extended = padded(with_rows, (("tm", 1),), 1)
    key_ext = to_tiles(extended[0], TH, TW)
    value_ext = to_tiles(extended[1], TH, TW)
    query_tiles = to_tiles(query_out.reshape(grid_shape), TH, TW)[0]
    tile_rows = row_count // TH
    attended = tile_attention(
        query_tiles,
        key_ext,
        value_ext,
        tile_offsets[:, 0],
        lax.axis_index("height") * tile_rows,
        lax.axis_index("tm") * frame_count,
        lax.axis_size("tm") * frame_count,
        lax.axis_size("height") * tile_rows,
    )
    self_mix = from_tiles(attended, TH, TW)
    self_out = jnp.dot(
        self_mix, w_full[:, 4 * head_width : 5 * head_width].T, preferred_element_type=jnp.float32
    )
    residual = flattened + modulation[2] * self_out
    normed = (layer_norm(residual) * cross_norm[0] + cross_norm[1]).astype(jnp.bfloat16)
    cross_query = rms_norm(
        jnp.dot(
            normed, w_full[:, 3 * head_width : 4 * head_width], preferred_element_type=jnp.float32
        ),
        norm_gains[2],
    ).astype(jnp.bfloat16)
    crossed = cross_attention(cross_query, text_key_set, text_value_set, text_mask)
    result = residual + jnp.dot(
        crossed, w_full[:, 5 * head_width :].T, preferred_element_type=jnp.float32
    )
    return result.astype(jnp.bfloat16).reshape(frame_count, row_count, col_count, model_dim)


def solution(mesh):
    placed = (
        P("tm", "height", None, None),
        P(),
        P(),
        P(),
        P("height", None),
        P(),
        P(None, "height"),
        P(None, "tm", "height", None, None),
        P(),
    )
    return jax.shard_map(
        body, mesh=mesh, in_specs=placed, out_specs=P("tm", "height", None, None), check_vma=False
    )
```

profile of v0, /device:TPU:1, one launch (start us, length us, event | category | flops | bytes accessed | tf_op | source)
XLA Modules:
  0.0 368.2 jit_solution(8702252480118346790)
XLA Ops:
  6.5 0.7 all-gather.3.cloned.1.call-update
  7.3 0.7 all-gather.5.cloned.1.call-update
  8.0 1.3 convert_reduce_fusion
  9.4 1.4 multiply_reduce_fusion.1
  10.8 1.5 slice_reduce_fusion.5
  12.3 1.5 slice_reduce_fusion.3
  13.8 125.2 %all-gather.3.cloned.1.call-done = bf16[1536,4608]{1,0:T(8,128)(2,1)} async-done(((bf16[48,4608]{1,0:T(8,128)(2,1)}), bf16[1536,4608]{1,0:T(8,128)(2,1)}) %all-gather.3.cloned.1.call-update) | async-done | bytes 14155792 | tf_op jit(solution)/shard_map/all_gather | solution.py:145
  139.1 5.0 %fusion.2 = f32[208,2304]{1,0:T(8,128)S(1)} fusion(bf16[1536,4608]{1,0:T(8,128)(2,1)} %all-gather.3.cloned.1.call-done, f32[1536]{0:T(1024)S(1)} %get-tuple-element.9, f32[1536]{0:T(1024)S(1)} %get-tuple-element.10, f32[208]{0:T(256)S(1)} %rsqrt.52, f32[208]{0:T(256)S(1)} %div.46, bf16[208,1536]{1,0:T(8,128)(2,1)} %bitcast.80), kind=kOutput, calls=%fused_computation.4 | convolution fusion | flops 1474117632 | bytes 9647744 | tf_op jit(solution)/shard_map/dot_general | solution.py:148
  144.3 0.9 multiply_convert_fusion.1
  145.2 0.9 pad_maximum_fusion.2
  146.1 2.3 collective-permute-start
  148.4 2.1 collective-permute-start.1
  151.0 0.7 broadcast_in_dim.53
  151.7 35.8 %collective-permute-done = bf16[2,1,2,104,768]{4,3,2,1,0:T(8,128)(2,1)S(1)} collective-permute-done((bf16[2,1,2,104,768]{4,3,2,1,0:T(8,128)(2,1)}, bf16[2,1,2,104,768]{4,3,2,1,0:T(8,128)(2,1)S(1)}, u32[]{:S(2)}, u32[]{:S(2)}) %collective-permute-start) | collective-permute-done | bytes 639008 | tf_op jit(solution)/shard_map/ppermute | solution.py:19
  187.5 1.5 pad_maximum_fusion.1
  189.0 2.6 collective-permute-start.2
  191.6 1.3 collective-permute-start.3
  192.9 0.6 compare_and_fusion
  193.5 0.6 pad_clamp_fusion
  194.1 0.6 broadcast_compare_fusion
  194.7 78.7 %all-gather.5.cloned.1.call-done = bf16[1536,1536]{0,1:T(8,128)(2,1)} async-done(((bf16[1536,48]{0,1:T(8,128)(2,1)}), bf16[1536,1536]{0,1:T(8,128)(2,1)}) %all-gather.5.cloned.1.call-update) | async-done | bytes 4718608 | tf_op jit(solution)/shard_map/all_gather | solution.py:137
  273.4 5.0 %convolution_convert_fusion = bf16[512,1536]{1,0:T(8,128)(2,1)S(1)} fusion(bf16[512,1536]{1,0:T(8,128)(2,1)S(1)} %copy-done, bf16[1536,1536]{0,1:T(8,128)(2,1)} %all-gather.5.cloned.1.call-done), kind=kOutput, calls=%fused_computation.9 | convolution fusion | flops 2416705536 | bytes 7864320 | tf_op jit(solution)/shard_map/dot_general | solution.py:138
  279.0 1.2 copy.40
  280.2 1.2 copy.39
  281.3 1.1 reshape_reshape.13
  282.6 0.9 reshape_squeeze_reshape.3
  283.5 3.1 pad_maximum_fusion
  286.7 2.8 fusion.73
  289.5 3.7 %reshape_squeeze.7 = bf16[3,3,2,4,26,768]{5,4,3,2,1,0:T(8,128)(2,1)S(1)} reshape(bf16[1,3,6,104,768]{4,3,2,1,0:T(8,128)(2,1)} %get-tuple-element.20) | data formatting | bytes 5750784 | tf_op jit(solution)/shard_map/reshape;squeeze | solution.py:39
  293.2 2.1 copy.48
  295.3 5.5 %reshape.220 = bf16[36,52,768]{2,1,0:T(8,128)(2,1)} reshape(bf16[3,3,4,2,26,768]{5,4,3,2,1,0:T(8,128)(2,1)} %copy.48) | data formatting | bytes 5750784 | tf_op jit(solution)/shard_map/reshape;reshape | solution.py:92
  300.9 3.7 %reshape_squeeze.6 = bf16[3,3,2,4,26,768]{5,4,3,2,1,0:T(8,128)(2,1)S(1)} reshape(bf16[1,3,6,104,768]{4,3,2,1,0:T(8,128)(2,1)} %get-tuple-element.19) | data formatting | bytes 5750784 | tf_op jit(solution)/shard_map/reshape;squeeze | solution.py:39
  304.6 2.2 copy.47
  306.8 5.7 %reshape.219 = bf16[36,52,768]{2,1,0:T(8,128)(2,1)} reshape(bf16[3,3,4,2,26,768]{5,4,3,2,1,0:T(8,128)(2,1)} %copy.47) | data formatting | bytes 5750784 | tf_op jit(solution)/shard_map/reshape;reshape | solution.py:96
  312.4 2.7 gather_fusion.1
  315.2 4.8 %gather_fusion = bf16[36,52,768]{2,1,0:T(8,128)(2,1)} fusion(bf16[36,52,768]{2,1,0:T(8,128)(2,1)} %reshape.219, s32[1024]{0:T(1024)} %pad_clamp_fusion), kind=kCustom, calls=%fused_computation.clone | custom fusion | bytes 5750928 | tf_op jit(solution)/shard_map/jit(_take)/gather | solution.py:95
  319.9 5.1 %broadcast_select_fusion.1 = (bf16[36,52,768]{2,1,0:T(8,128)(2,1)}, bf16[36,52,768]{2,1,0:T(8,128)(2,1)}) fusion(bf16[36,52,768]{2,1,0:T(8,128)(2,1)} %gather_fusion, pred[36]{0:T(512)(128)(4,1)S(1)} %copy-done.12, bf16[36,52,768]{2,1,0:T(8,128)(2,1)S(1)} %copy-done.3), kind=kLoop, calls=%fused_computation.8 | loop fusion | flops 2875392 | bytes 11501604 | tf_op jit(solution)/shard_map/jit(_take)/select_n | solution.py:95
  325.0 6.9 %reshape.186 = bf16[4,468,6,128]{3,2,1,0:T(8,128)(2,1)} reshape(bf16[36,52,768]{2,1,0:T(8,128)(2,1)} %get-tuple-element.26) | data formatting | bytes 5750784 | tf_op jit(solution)/shard_map/reshape | solution.py:92
  332.0 4.8 %reshape.185 = bf16[4,468,6,128]{3,2,1,0:T(8,128)(2,1)} reshape(bf16[36,52,768]{2,1,0:T(8,128)(2,1)S(1)} %copy-done.4) | data formatting | bytes 5750784 | tf_op jit(solution)/shard_map/reshape | solution.py:97
  336.8 3.9 %fusion.6 = f32[4,6,52,468]{3,2,1,0:T(8,128)S(1)} fusion(bf16[4,468,6,128]{3,2,1,0:T(8,128)(2,1)} %reshape.186, bf16[4,52,6,128]{3,2,0,1:T(8,128)(2,1)S(1)} %copy-done.6), kind=kOutput, calls=%fused_computation.12 | convolution fusion | flops 149520384 | bytes 5531136 | tf_op jit(solution)/shard_map/tphd,tkhd->thpk/dot_general | solution.py:100
  340.7 0.9 fusion.74
  341.6 4.6 %fusion.31 = bf16[4,52,6,128]{3,1,2,0:T(8,128)(2,1)S(1)} fusion(f32[4,6,52]{2,1,0:T(8,128)S(1)} %fusion.74, bf16[4,468,6,128]{3,2,1,0:T(8,128)(2,1)} %reshape.185, f32[4,6,52,468]{3,2,1,0:T(8,128)S(1)} %fusion.6, pred[4,468]{1,0:T(4,128)(4,1)S(1)} %copy-done.13), kind=kOutput, calls=%fused_computation.50 | convolution fusion | flops 152602160 | bytes 5538000 | tf_op jit(solution)/shard_map/thpk,tkhd->tphd/dot_general | solution.py:107
  346.6 0.6 copy-done.5
  347.2 2.7 fusion.75
  350.2 2.6 multiply_reduce_fusion.2
  352.8 1.0 fusion.76
  353.9 4.1 %fusion.34 = bf16[6,26,8,128]{3,2,1,0:T(8,128)(2,1)S(1)} fusion(bf16[512,6,128]{0,2,1:T(8,128)(2,1)} %bitcast.86, f32[6,208]{1,0:T(8,128)S(1)} %fusion.76, pred[512]{0:T(512)(128)(4,1)S(1)} %copy-done.15, bf16[512,6,128]{0,2,1:T(8,128)(2,1)} %bitcast.84, f32[208,768]{1,0:T(8,128)} %copy-done.16, f32[768]{0:T(1024)S(1)} %copy-done.11, ...), kind=kOutput, calls=%fused_computation.51 | convolution fusion | flops 330991328 | bytes 2540736 | tf_op jit(solution)/shard_map/tgp,ptr->gtr/dot_general | solution.py:126
  358.0 3.4 fusion.9
  (66 shorter events, 2.5 us)
Async XLA Ops:
  6.5 266.9 %copy-start = (bf16[512,1536]{1,0:T(8,128)(2,1)S(1)}, bf16[512,1536]{1,0:T(8,128)(2,1)}, u32[]{:S(2)}) copy-start(bf16[512,1536]{1,0:T(8,128)(2,1)} %param.16) | copy-start | bytes 4718596
  6.5 132.5 %all-gather.3.cloned.1.call-start = ((), (), s32[]{:S(2)}) async-start(), calls=%async_computation | async-start | bytes 14598144 | tf_op jit(solution)/shard_map/all_gather | solution.py:145
  7.3 266.2 %all-gather.5.cloned.1.call-start = ((), (), s32[]{:S(2)}) async-start(), calls=%async_computation.1 | async-start | bytes 4866048 | tf_op jit(solution)/shard_map/all_gather | solution.py:137
  144.1 6.4 %copy-start.8 = (s32[3,1,1,4,8]{4,3,2,1,0:T(4,128)S(1)}, s32[3,1,1,4,8]{4,3,2,1,0:T(4,128)}, u32[]{:S(2)}) copy-start(s32[3,1,1,4,8]{4,3,2,1,0:T(4,128)} %param.18) | copy-start | bytes 1156
  145.2 48.9 %copy-start.9 = (f32[2,1536]{1,0:T(2,128)S(1)}, f32[2,1536]{1,0:T(2,128)}, u32[]{:S(2)}) copy-start(f32[2,1536]{1,0:T(2,128)} %param.13) | copy-start | bytes 36868
  145.2 48.9 %copy-start.14 = (s32[512]{0:T(512)S(1)}, s32[512]{0:T(512)}, u32[]{:S(2)}) copy-start(s32[512]{0:T(512)} %param.19) | copy-start | bytes 6148
  146.1 41.4 %collective-permute-start = (bf16[2,1,2,104,768]{4,3,2,1,0:T(8,128)(2,1)}, bf16[2,1,2,104,768]{4,3,2,1,0:T(8,128)(2,1)S(1)}, u32[]{:S(2)}, u32[]{:S(2)}) collective-permute-start(bf16[2,1,2,104,768]{4,3,2,1,0:T(8,128)(2,1)} %pad_maximum_fusion.2), channel_id=1, source_target_pairs={{0,1},{1,2},{2,3},{3,4},{4,5},{5,6},{6,7},{7,8},{8,9},{9,10},{10,1... | collective-permute-start | bytes 1916936 | tf_op jit(solution)/shard_map/ppermute | solution.py:19
  148.4 39.1 %collective-permute-start.1 = (bf16[2,1,2,104,768]{4,3,2,1,0:T(8,128)(2,1)}, bf16[2,1,2,104,768]{4,3,2,1,0:T(8,128)(2,1)S(1)}, u32[]{:S(2)}, u32[]{:S(2)}) collective-permute-start(bf16[2,1,2,104,768]{4,3,2,1,0:T(8,128)(2,1)} %pad_maximum_fusion.2), channel_id=1, source_target_pairs={{1,0},{2,1},{3,2},{4,3},{5,4},{6,5},{7,6},{8,7},{9,8},{10,9},{11,1... | collective-permute-start | bytes 1916936 | tf_op jit(solution)/shard_map/ppermute | solution.py:20
  189.0 94.6 %collective-permute-start.2 = (bf16[2,1,6,104,768]{4,3,2,1,0:T(8,128)(2,1)}, bf16[2,1,6,104,768]{4,3,2,1,0:T(8,128)(2,1)}, u32[]{:S(2)}, u32[]{:S(2)}) collective-permute-start(bf16[2,1,6,104,768]{4,3,2,1,0:T(8,128)(2,1)} %pad_maximum_fusion.1), channel_id=1, source_target_pairs={{0,32},{32,64},{64,96},{96,128},{128,160},{160,192},{192,224},{1,3... | collective-permute-start | bytes 5750792 | tf_op jit(solution)/shard_map/ppermute | solution.py:19
  191.6 92.0 %collective-permute-start.3 = (bf16[2,1,6,104,768]{4,3,2,1,0:T(8,128)(2,1)}, bf16[2,1,6,104,768]{4,3,2,1,0:T(8,128)(2,1)}, u32[]{:S(2)}, u32[]{:S(2)}) collective-permute-start(bf16[2,1,6,104,768]{4,3,2,1,0:T(8,128)(2,1)} %pad_maximum_fusion.1), channel_id=1, source_target_pairs={{32,0},{64,32},{96,64},{128,96},{160,128},{192,160},{224,192},{33,... | collective-permute-start | bytes 5750792 | tf_op jit(solution)/shard_map/ppermute | solution.py:20
  306.8 5.7 %copy-start.2 = (bf16[36,52,768]{2,1,0:T(8,128)(2,1)S(1)}, bf16[36,52,768]{2,1,0:T(8,128)(2,1)}, u32[]{:S(2)}) copy-start(bf16[36,52,768]{2,1,0:T(8,128)(2,1)} %reshape.220) | copy-start | bytes 8626180
  315.2 4.8 %copy-start.3 = (bf16[36,52,768]{2,1,0:T(8,128)(2,1)S(1)}, bf16[36,52,768]{2,1,0:T(8,128)(2,1)}, u32[]{:S(2)}) copy-start(bf16[36,52,768]{2,1,0:T(8,128)(2,1)} %gather_fusion.1) | copy-start | bytes 8626180
  315.2 4.8 %copy-start.12 = (pred[36]{0:T(512)(128)(4,1)S(1)}, pred[36]{0:T(512)(128)(4,1)}, u32[]{:S(2)}) copy-start(pred[36]{0:T(512)(128)(4,1)} %get-tuple-element.17) | copy-start | bytes 112
  325.0 6.9 %copy-start.4 = (bf16[36,52,768]{2,1,0:T(8,128)(2,1)S(1)}, bf16[36,52,768]{2,1,0:T(8,128)(2,1)}, u32[]{:S(2)}) copy-start(bf16[36,52,768]{2,1,0:T(8,128)(2,1)} %get-tuple-element.25) | copy-start | bytes 8626180
  332.0 4.8 %copy-start.6 = (bf16[4,52,6,128]{3,2,0,1:T(8,128)(2,1)S(1)}, bf16[4,52,6,128]{3,2,0,1:T(8,128)(2,1)}, u32[]{:S(2)}) copy-start(bf16[4,52,6,128]{3,2,0,1:T(8,128)(2,1)} %reshape_squeeze_reshape.3) | copy-start | bytes 958468
  336.8 3.9 %copy-start.13 = (pred[4,468]{1,0:T(4,128)(4,1)S(1)}, pred[4,468]{1,0:T(4,128)(4,1)}, u32[]{:S(2)}) copy-start(pred[4,468]{1,0:T(4,128)(4,1)} %broadcast_in_dim.53) | copy-start | bytes 5620
  346.2 1.1 copy-start.5
  346.2 1.1 copy-start.10
  350.2 2.6 copy-start.7
  350.2 2.6 copy-start.11
  350.2 2.6 copy-start.15
  352.8 1.1 copy-start.16
  353.9 7.5 %copy-start.1 = (bf16[512,1536]{1,0:T(8,128)(2,1)S(1)}, bf16[512,1536]{1,0:T(8,128)(2,1)}, u32[]{:S(2)}) copy-start(bf16[512,1536]{1,0:T(8,128)(2,1)} %param.16) | copy-start | bytes 4718596
Sparse Core Ops, SparseCore 0:
  10.1 128.8 all-gather.2
  141.8 131.5 all-gather.4
where the time goes:
time: 369 us; the launch traced here: 368 us
  waiting for transfers between devices  241 us (65%)
  local copies, waits for them, and re-layouts  53.4 us (14%)
  matrix products  32.2 us (9%)
  other arithmetic  19.4 us (5%)
  between operations  13.7 us (4%)
  starting transfers between devices  8.29 us (2%)
    all_gather x1, waiting for transfers between devices, body(): w_full = lax.all_gather(w_main, 'height', axis=0, tiled=True)  125 us
    all_gather x1, waiting for transfers between devices, body(): text_cols = lax.all_gather(w_text, 'height', axis=1, tiled=True)  78.7 us
    ppermute x2, waiting for transfers between devices, padded(): before = lax.ppermute(last, axis, up)  35.8 us
    another operation x3, local copies, waits for them, and re-layouts, to_tiles(): field_in.reshape(frame_count, row_count // tile_height, tile_height, col_...  8.5 us
    another operation x2, local copies, waits for them, and re-layouts, tile_attention(): value_ext.reshape(-1, cell_count, head_width)  7.83 us
    another operation x2, local copies, waits for them, and re-layouts, tile_attention(): key_ext.reshape(-1, cell_count, head_width)  7.65 us
  transfers between devices with their start and end apart: 6, of which 3 were waited for; matrix products, arithmetic and copies ran while one was open for 7% of the time, Pallas kernels for 0%

commit v1 on v0

v1 whole, which is shorter than its diff:
```python
import jax
import jax.numpy as jnp
from jax import lax
from jax.experimental import pallas as pl
from jax.experimental.pallas import tpu as pltpu
from jax.sharding import PartitionSpec as P

MESH = pl.DeviceIdType.MESH
BF = jnp.bfloat16
F32 = jnp.float32
TOK = 208
WIN = 640
HALF = 384
D = 1536
SCALE = 128.0**-0.5 * 1.4426950408889634
K0, V0, Q0, SO0, CQ0, TX0, CO0, END = 0, 384, 768, 1152, 1536, 1920, 2176, 2560
NSEM = 160


def layer_norm(values):
    average = jnp.mean(values, axis=-1, keepdims=True)
    centred = values - average
    variance = jnp.mean(centred * centred, axis=-1, keepdims=True)
    return centred * lax.rsqrt(variance + 1e-06)


def dot_nt(a, b):
    return lax.dot_general(a, b, (((1,), (1,)), ((), ())), preferred_element_type=F32)


def dot(a, b):
    return jnp.dot(a, b, preferred_element_type=F32)


def kernel(
    lat, mod, cn, ng, w, ts, wt, off, tmask, out,
    ga, gb, oth, modb, kvb, raw, ssb, qb, rb, mb, mixb, mixo, res, txt,
    send, recv,
):
    t = lax.axis_index("tm")
    h = lax.axis_index("height")
    c = lax.rem(h, 2)
    yhi = lax.rem(lax.div(h, 2), 2)
    z = lax.div(h, 4)
    x = lax.div(t, 2)
    ylo = lax.rem(t, 2)

    def at(dt, dh):
        return (lax.rem(t + dt + 8, 8), lax.rem(h + dh + 32, 32))

    hs = h + 1 - 2 * c
    sib = (t, hs)
    pt, ph = t + 1 - 2 * ylo, h + 2 - 4 * yhi
    pho = ph + 1 - 2 * c
    zup, zdn, xup, xdn = at(0, 4), at(0, -4), at(2, 0), at(-2, 0)
    halo = [(dt, dg) for dt in (-1, 0, 1) for dg in (-1, 0, 1) if (dt, dg) != (0, 0)]
    peers = [sib, (pt, ph), (pt, pho), zup, zdn, xup, xdn]
    peers += [at(dt, 2 * dg) for dt, dg in halo]

    def rows(start, count):
        return pl.ds(pl.multiple_of(start, 16), count)

    own = rows(48 * h, 48)
    for part, col in ((1, K0), (2, V0), (0, Q0), (4, SO0), (3, CQ0), (5, CO0)):
        mine = pl.ds(pl.multiple_of(768 * part + HALF * c, 128), HALF)
        other = pl.ds(pl.multiple_of(768 * part + HALF * (1 - c), 128), HALF)
        ga[own, pl.ds(col, HALF)] = w[:, mine]
        oth[:, pl.ds(col, HALF)] = w[:, other]

    barrier = pltpu.get_barrier_semaphore()
    for peer in peers:
        pl.semaphore_signal(barrier, inc=1, device_id=peer, device_id_type=MESH)
    pl.semaphore_wait(barrier, len(peers))

    used = [0]
    started = []

    def push(src, dst, peer, arriving):
        i = used[0]
        used[0] += 1
        copy = pltpu.make_async_remote_copy(
            src_ref=src, dst_ref=dst, send_sem=send.at[i], recv_sem=recv.at[i],
            device_id=peer, device_id_type=MESH,
        )
        copy.start()
        started.append(copy)
        arrival = pltpu.make_async_remote_copy(
            src_ref=arriving, dst_ref=arriving, send_sem=send.at[i], recv_sem=recv.at[i],
            device_id=peer, device_id_type=MESH,
        )
        return arrival.wait_recv

    slab_waits = {}

    def slab(lo, hi):
        cols = pl.ds(lo, hi - lo)
        slab_waits[lo] = [
            push(oth.at[:, cols], ga.at[own, cols], sib, ga.at[rows(48 * hs, 48), cols]),
            push(ga.at[own, cols], ga.at[own, cols], (pt, ph), ga.at[rows(48 * ph, 48), cols]),
            push(oth.at[:, cols], ga.at[own, cols], (pt, pho), ga.at[rows(48 * pho, 48), cols]),
        ]

    def slab_wait(lo):
        for wait in slab_waits[lo]:
            wait()

    def slot(step):
        return 192 * lax.rem(z + step + 8, 8)

    def ring_z(lo, hi, forward):
        cols = pl.ds(lo, hi - lo)
        slab_wait(lo)
        for s in range(4):
            a, n, b = (0, 192, 0) if s < 3 else (0, 96, 96)

            def view(step, base):
                return ga.at[rows(slot(step) + base, n), cols]

            up = push(view(-s, a), view(-s, a), zup, view(-s - 1, a))
            dn = push(view(s, b), view(s, b), zdn, view(s + 1, b))
            yield
            up()
            dn()
        yield from finish(lo, hi, forward)

    def finish(lo, hi, forward):
        if forward:
            cols, there = pl.ds(lo, hi - lo), pl.ds(lo - SO0, hi - lo)
            wait = push(ga.at[:, cols], gb.at[:, there], sib, gb.at[:, there])
            yield
            wait()

    def ring_x(lo, hi, forward):
        cols = pl.ds(lo, hi - lo)
        slab_wait(lo)

        def piece(step, quarter):
            return ga.at[rows(slot(step) + 48 * quarter, 48), cols]

        for s in range(4):
            if s < 3:
                up = push(piece(-s, x), piece(-s, x), zup, piece(-s - 1, x))
                dn = push(piece(s, x), piece(s, x), zdn, piece(s + 1, x))
                yield
                up()
                dn()
            else:
                up = push(piece(-s, x), piece(-s, x), zup, piece(-s - 1, x))
                yield
                up()
        left, right = lax.rem(x + 3, 4), lax.rem(x + 1, 4)

        def fan(quarter, slabs, peer, count):
            i = used[0]
            used[0] += 1

            def one(k, carry):
                part = piece(k, quarter)
                pltpu.make_async_remote_copy(
                    src_ref=part, dst_ref=part, send_sem=send.at[i], recv_sem=recv.at[i],
                    device_id=peer, device_id_type=MESH,
                ).start()
                return carry

            lax.fori_loop(slabs[0], slabs[1], one, 0)
            whole = ga.at[pl.ds(0, 48 * count), cols]
            copy = pltpu.make_async_remote_copy(
                src_ref=whole, dst_ref=whole, send_sem=send.at[i], recv_sem=recv.at[i],
                device_id=peer, device_id_type=MESH,
            )
            started.append(copy)
            return copy.wait_recv

        to_up = fan(x, (1, 8), xup, 7)
        to_dn = fan(x, (1, 8), xdn, 7)
        yield
        to_up()
        to_dn()
        to_up = fan(left, (1, 5), xup, 4)
        to_dn = fan(right, (5, 8), xdn, 3)
        yield
        to_up()
        to_dn()
        yield from finish(lo, hi, forward)

    chunks = ((K0, V0), (V0, Q0), (Q0, SO0), (SO0, CQ0))
    for lo, hi in chunks:
        slab(lo, hi)

    ring_k, ring_v = ring_z(K0, V0, False), ring_z(V0, Q0, False)
    ring_q, ring_so = ring_x(Q0, SO0, False), ring_z(SO0, CQ0, True)
    ring_cq, ring_co = ring_x(CQ0, CO0, True), ring_x(CO0, END, True)

    def pump(*rings):
        for ring in rings:
            next(ring, None)

    def drain(*rings):
        for ring in rings:
            for _ in ring:
                pass

    pump(ring_k, ring_v, ring_q)

    mine = rows(TOK * c, TOK)
    theirs = rows(TOK * (1 - c), TOK)
    latent = lat[...].astype(F32)
    modb[mine, :] = (layer_norm(latent) * (1.0 + mod[1:2, :]) + mod[0:1, :]).astype(BF)
    got_mod = push(modb.at[mine, :], modb.at[mine, :], sib, modb.at[theirs, :])

    txt[...] = dot_nt(wt[...], ts[...]).astype(BF)
    ga[own, pl.ds(TX0, 256)] = txt[:, pl.ds(pl.multiple_of(256 * c, 128), 256)]
    oth[:, pl.ds(TX0, 256)] = txt[:, pl.ds(pl.multiple_of(256 * (1 - c), 128), 256)]
    slab(CQ0, CO0)
    slab(CO0, END)
    pump(ring_k, ring_v, ring_q)

    lane = lax.broadcasted_iota(jnp.int32, (8, WIN), 1)
    frame = lax.broadcasted_iota(jnp.int32, (8, WIN), 0)

    def step_of(value, *edges):
        total = jnp.zeros_like(value)
        for edge in edges:
            total = total + (value >= edge).astype(jnp.int32)
        return total

    row_at = step_of(lane, 208, 416)
    within = lane - 208 * row_at
    within = within - 104 * step_of(within, 104)
    code = jnp.where(lane < 624, 12 * frame + 4 * row_at + step_of(within, 26, 52, 78), -2)
    for q in range(4):
        allowed = code == 16 + q
        for j in range(8):
            dt, dr, dc = off[0, 0, 0, q, j], off[1, 0, 0, q, j], off[2, 0, 0, q, j]
            ft, rt, ct = t + dt, h + dr, q + dc
            usable = (ft >= 0) & (ft < 8) & (rt >= 0) & (rt < 32) & (ct >= 0) & (ct < 4)
            target = jnp.where(usable, 12 * (dt + 1) + 4 * (dr + 1) + ct, -1)
            allowed = allowed | (code == target)
        rb[c, pl.ds(8 * q, 8), :] = jnp.where(allowed, 0.0, -jnp.inf).astype(F32)
    got_rb = push(rb.at[c], rb.at[c], sib, rb.at[1 - c])
    pump(ring_k, ring_v, ring_q)
    got_rb()
    token = lax.broadcasted_iota(jnp.int32, (TOK, 1), 0)
    token = token - 104 * step_of(token, 104)
    tile = step_of(token, 26, 52, 78)

    def masks(i, carry):
        r, f = lax.div(i, 3), lax.rem(i, 3)
        picked = rb[r, pl.ds(f, 1), :]
        for q in range(1, 4):
            picked = jnp.where(tile == q, rb[r, pl.ds(8 * q + f, 1), :], picked)
        mb[r, f] = jnp.broadcast_to(picked, (TOK, WIN))
        return carry

    lax.fori_loop(0, 6, masks, 0)
    for f in range(3):
        kvb[f, pl.ds(832, 16), :] = jnp.zeros((16, 768), BF)
    pump(ring_k, ring_v, ring_q)
    got_mod()
    drain(ring_k, ring_v)
    pump(ring_so, ring_cq, ring_co)

    both = pl.ds(TOK, 2 * TOK)
    raw[...] = dot(modb[...], ga[:, pl.ds(K0, HALF)])

    def squares(i):
        ssb[i, 0] = jnp.broadcast_to(
            jnp.sum(raw[...] * raw[...], axis=-1, keepdims=True), (2 * TOK, 128)
        )
        return push(ssb.at[i, 0], ssb.at[i, 1], sib, ssb.at[i, 1])

    def gain(i, half):
        return ng[i : i + 1, pl.ds(pl.multiple_of(HALF * half, 128), HALF)]

    def normal(i, gains):
        total = ssb[i, 0, :, 0:1] + ssb[i, 1, :, 0:1]
        return raw[...] * lax.rsqrt(total * (1.0 / 768) + 1e-06) * gains

    def send_halo(lo):
        cols = pl.ds(lo, HALF)
        waits = []
        for dt, dg in halo:
            first, count = (TOK, 2 * TOK) if dg == 0 else (2 * TOK, TOK) if dg > 0 else (TOK, TOK)
            there = TOK if dg == 0 else 0 if dg > 0 else 3 * TOK
            src = kvb.at[1, pl.ds(first, count), cols]
            dst = kvb.at[1 - dt, pl.ds(there, count), cols]
            waits.append(push(src, dst, at(dt, 2 * dg), dst))
        return waits

    got_k_squares = squares(0)
    kvb[1, both, pl.ds(HALF, HALF)] = dot(modb[...], ga[:, pl.ds(V0, HALF)]).astype(BF)
    v_waits = send_halo(HALF)
    got_k_squares()
    kvb[1, both, pl.ds(0, HALF)] = normal(0, gain(1, c)).astype(BF)
    k_waits = send_halo(0)

    drain(ring_q)
    pump(ring_so, ring_cq, ring_co)
    raw[...] = dot(modb[...], ga[:, pl.ds(Q0, HALF)])
    got_q_squares = squares(1)
    pump(ring_so, ring_cq, ring_co)
    got_q_squares()
    qb[...] = normal(1, gain(0, c) * SCALE).astype(BF)
    for _ in range(4):
        pump(ring_so, ring_cq, ring_co)
    for wait in v_waits + k_waits:
        wait()

    def attend(r, i):
        q = qb[pl.ds(TOK * r, TOK), pl.ds(128 * i, 128)]
        keys = pl.ds(TOK * r, WIN)
        scores = [dot_nt(q, kvb[f, keys, pl.ds(128 * i, 128)]) + mb[r, f] for f in range(3)]
        largest = jnp.max(scores[0], axis=-1, keepdims=True)
        for s in scores[1:]:
            largest = jnp.maximum(largest, jnp.max(s, axis=-1, keepdims=True))
        total, mixed = 0.0, 0.0
        for f in range(3):
            p = jnp.exp2(scores[f] - largest)
            total = total + jnp.sum(p, axis=-1, keepdims=True)
            mixed = mixed + dot(p.astype(BF), kvb[f, keys, pl.ds(HALF + 128 * i, 128)])
        mixb[pl.ds(TOK * r, TOK), pl.ds(128 * i, 128)] = (mixed / total).astype(BF)

    for r in range(2):
        for i in range(3):
            attend(r, i)
            pump(ring_so, ring_cq, ring_co)
    got_mix = push(mixb.at[theirs, :], mixo, sib, mixo)
    drain(ring_so)
    got_mix()

    def outward(mine_in, other_in, lo, i):
        n = pl.ds(pl.multiple_of(256 * i, 256), 256)
        return dot_nt(mine_in, ga[n, pl.ds(lo, HALF)]) + dot_nt(
            other_in, gb[n, pl.ds(lo - SO0, HALF)]
        )

    mix_mine, mix_other = mixb[mine, :], mixo[...]

    def self_out(i, carry):
        n = pl.ds(pl.multiple_of(256 * i, 256), 256)
        res[:, n] = lat[:, n].astype(F32) + mod[2:3, n] * outward(mix_mine, mix_other, SO0, i)
        return carry

    lax.fori_loop(0, 6, self_out, 0)
    drain(ring_cq)
    normed = (layer_norm(res[...]) * cn[0:1, :] + cn[1:2, :]).astype(BF)
    cq_mine = dot(normed, ga[:, pl.ds(CQ0, HALF)])
    cq_other = dot(normed, gb[:, pl.ds(CQ0 - SO0, HALF)])
    square = jnp.sum(cq_mine * cq_mine, axis=-1, keepdims=True)
    square = square + jnp.sum(cq_other * cq_other, axis=-1, keepdims=True)
    inverse = lax.rsqrt(square * (1.0 / 768) + 1e-06) * SCALE
    raw[0:TOK, :] = cq_mine * inverse * (gain(2, c) * gain(3, c))
    raw[TOK : 2 * TOK, :] = cq_other * inverse * (gain(2, 1 - c) * gain(3, 1 - c))

    def text_scale(ref, lo):
        keys = ref[0:768, pl.ds(lo, 256)].astype(F32)
        return lax.rsqrt(jnp.sum(keys * keys, axis=0, keepdims=True) * (1.0 / 768) + 1e-06)

    real = [tmask[pl.ds(c, 1), :] == 1, tmask[pl.ds(1 - c, 1), :] == 1]
    parts = [(ga, TX0), (gb, TX0 - SO0)]
    scales = [text_scale(*part) for part in parts]
    for k in range(2):
        base = HALF * c if k == 0 else HALF * (1 - c)
        for i in range(3):
            q = raw[pl.ds(TOK * k, TOK), pl.ds(128 * i, 128)].astype(BF)
            krow, vrow = rows(base + 128 * i, 128), rows(768 + base + 128 * i, 128)
            scores = [
                jnp.where(real[j], dot(q, ref[krow, pl.ds(lo, 256)]) * scales[j], -jnp.inf)
                for j, (ref, lo) in enumerate(parts)
            ]
            largest = jnp.maximum(
                jnp.max(scores[0], axis=-1, keepdims=True),
                jnp.max(scores[1], axis=-1, keepdims=True),
            )
            total, mixed = 0.0, 0.0
            for j, (ref, lo) in enumerate(parts):
                p = jnp.exp2(scores[j] - largest)
                total = total + jnp.sum(p, axis=-1, keepdims=True)
                mixed = mixed + dot_nt(p.astype(BF), ref[vrow, pl.ds(lo, 256)])
            qb[pl.ds(TOK * k, TOK), pl.ds(128 * i, 128)] = (mixed / total).astype(BF)
    drain(ring_co)
    cross_mine, cross_other = qb[0:TOK, :], qb[TOK : 2 * TOK, :]

    def cross_out(i, carry):
        n = pl.ds(pl.multiple_of(256 * i, 256), 256)
        out[:, n] = (res[:, n] + outward(cross_mine, cross_other, CO0, i)).astype(BF)
        return carry

    lax.fori_loop(0, 6, cross_out, 0)
    for copy in started:
        copy.wait_send()


def body(
    latent, modulation, cross_norm, norm_gains, w_main, text_states, w_text, tile_offsets, text_mask
):
    vmem = pl.BlockSpec(memory_space=pltpu.VMEM)
    smem = pl.BlockSpec(memory_space=pltpu.SMEM)
    result = pl.pallas_call(
        kernel,
        out_shape=jax.ShapeDtypeStruct((TOK, D), BF),
        in_specs=[vmem] * 7 + [smem, vmem],
        out_specs=vmem,
        scratch_shapes=[
            pltpu.VMEM((D, END), BF),
            pltpu.VMEM((D, END - SO0), BF),
            pltpu.VMEM((48, END), BF),
            pltpu.VMEM((2 * TOK, D), BF),
            pltpu.VMEM((3, 848, 768), BF),
            pltpu.VMEM((2 * TOK, HALF), F32),
            pltpu.VMEM((2, 2, 2 * TOK, 128), F32),
            pltpu.VMEM((2 * TOK, HALF), BF),
            pltpu.VMEM((2, 32, WIN), F32),
            pltpu.VMEM((2, 3, TOK, WIN), F32),
            pltpu.VMEM((2 * TOK, HALF), BF),
            pltpu.VMEM((TOK, HALF), BF),
            pltpu.VMEM((TOK, D), F32),
            pltpu.VMEM((48, 512), BF),
            pltpu.SemaphoreType.DMA((NSEM,)),
            pltpu.SemaphoreType.DMA((NSEM,)),
        ],
        compiler_params=pltpu.CompilerParams(
            collective_id=0, has_side_effects=True, vmem_limit_bytes=60 * 1024 * 1024
        ),
        cost_estimate=pl.CostEstimate(
            flops=6_000_000_000, bytes_accessed=6_000_000, transcendentals=3_000_000
        ),
    )(
        latent.reshape(TOK, D),
        modulation,
        cross_norm,
        norm_gains,
        w_main,
        text_states,
        w_text.T,
        tile_offsets,
        text_mask.reshape(2, 256),
    )
    return result.reshape(latent.shape)


def solution(mesh):
    placed = (
        P("tm", "height", None, None),
        P(),
        P(),
        P(),
        P("height", None),
        P(),
        P(None, "height"),
        P(None, "tm", "height", None, None),
        P(),
    )
    return jax.shard_map(
        body, mesh=mesh, in_specs=placed, out_specs=P("tm", "height", None, None), check_vma=False
    )
```

time: 369 us -> 153 us (0.41)
  waiting for transfers between devices: 241 us -> 0 us
  Pallas kernels: 0 us -> 147 us
  local copies, waits for them, and re-layouts: 53.4 us -> 3.22 us
  matrix products: 32.2 us -> 0 us
  other arithmetic: 19.4 us -> 0 us
  between operations: 13.7 us -> 0.01 us
  starting transfers between devices: 8.29 us -> 0 us
    all_gather x2 -> x0, waiting for transfers between devices: 204 us -> none  [the longest x1 125 us: body(): w_full = lax.all_gather(w_main, 'height', axis=0, tiled=True)]
    pallas_call x0 -> x1, Pallas kernels: none -> 147 us  [body(): pl.pallas_call(kernel, out_shape=jax.ShapeDtypeStruct((TOK, D), BF), in_s...]
    ppermute x4 -> x0, waiting for transfers between devices: 35.8 us -> none  [the longest x2 35.8 us: padded(): before = lax.ppermute(last, axis, up)]
    dot_general x8 -> x0, matrix products: 31.2 us -> none  [the longest x1 5.02 us: body(): jnp.dot(modulated, w_full[:, :3 * head_width], preferred_element_type=jnp...]
    another operation x9 -> x0, local copies, waits for them, and re-layouts: 25 us -> none  [the longest x3 8.5 us: to_tiles(): field_in.reshape(frame_count, row_count // tile_height, tile_height, col_...]
    reshape x3 -> x1, local copies, waits for them, and re-layouts: 11.8 us -> 1.27 us  [body(): text_mask.reshape(2, 256)]
    ppermute x4 -> x0, starting transfers between devices: 8.25 us -> none  [the longest x2 4.89 us: padded(): before = lax.ppermute(last, axis, up)]
    gather x2 -> x0, local copies, waits for them, and re-layouts: 7.5 us -> none  [the longest x1 4.76 us: tile_attention(): jnp.take(value_ext.reshape(-1, cell_count, head_width), position, axis=0)]
  transfers between devices with their start and end apart: 6 -> 0, of which waited for: 3 -> 0; matrix products, arithmetic and copies ran while one was open for 7% -> 0% of each run, Pallas kernels for 0% -> 0%
where the time goes in v1:
time: 153 us; the launch traced here: 150 us
  Pallas kernels  147 us (96%)
  local copies, waits for them, and re-layouts  3.22 us (2%)
    pallas_call x1, Pallas kernels, body(): pl.pallas_call(kernel, out_shape=jax.ShapeDtypeStruct((TOK, D), BF), in_s...  147 us

profile of v1, /device:TPU:1, one launch (start us, length us, event | category | flops | bytes accessed | tf_op | source)
XLA Modules:
  0.0 149.9 jit_solution(4989571412785619817)
XLA Ops:
  0.0 1.3 reshape.10.tmask
  1.3 146.6 %shard_map.91 = bf16[208,1536]{1,0:T(8,128)(2,1)} custom-call(bf16[208,1536]{1,0:T(8,128)(2,1)} %bitcast.4, f32[3,1536]{1,0:T(4,128)} %mod.1, f32[2,1536]{1,0:T(2,128)} %cn.1, f32[4,768]{1,0:T(4,128)} %ng.1, bf16[48,4608]{1,0:T(8,128)(2,1)} %w.1, bf16[512,1536]{1,0:T(8,128)(2,1)} %ts.1, bf16[48,1536]{1,0:T(8,128)(2,1)} %bitcast.5, s32[3,1,1,4,8]{4,3,2,1,0:T(4,128)} %off.1, ...), custom_call_target="tpu_custom_call" | custom-call | flops 6000000000 | bytes 6000000 | tf_op jit(solution)/shard_map/pallas_call | solution.py:399
  147.9 2.0 %copy.11 = bf16[1,2,104,1536]{3,2,1,0:T(8,128)(2,1)} copy(bf16[1,2,104,1536]{3,2,1,0:T(8,128)(2,1)} %bitcast.3) | data formatting | bytes 1277952

commit v2 on v1

--- a/solution.py
+++ b/solution.py
@@ -33,9 +33,9 @@
 
 
 def kernel(
-    lat, mod, cn, ng, w, ts, wt, off, tmask, out,
-    ga, gb, oth, modb, kvb, raw, ssb, qb, rb, mb, mixb, mixo, res, txt,
-    send, recv,
+    lat_in, mod, cn, ng, w_in, ts_in, wt_in, off, tmask, out,
+    lat, w, ts, wt, ga, gb, oth, modb, lats, kvb, kraw, ssb, raw, ssq, qb, rb, mb, mixb, mixo, res, txt,
+    send, recv, load,
 ):
     t = lax.axis_index("tm")
     h = lax.axis_index("height")
@@ -45,6 +45,13 @@
     x = lax.div(t, 2)
     ylo = lax.rem(t, 2)
 
+    loads = [
+        pltpu.make_async_copy(src, dst, load.at[i])
+        for i, (src, dst) in enumerate(((w_in, w), (lat_in, lat), (wt_in, wt), (ts_in, ts)))
+    ]
+    for copy in loads:
+        copy.start()
+
     def at(dt, dh):
         return (lax.rem(t + dt + 8, 8), lax.rem(h + dh + 32, 32))
 
@@ -53,42 +60,52 @@
     pt, ph = t + 1 - 2 * ylo, h + 2 - 4 * yhi
     pho = ph + 1 - 2 * c
     zup, zdn, xup, xdn = at(0, 4), at(0, -4), at(2, 0), at(-2, 0)
-    halo = [(dt, dg) for dt in (-1, 0, 1) for dg in (-1, 0, 1) if (dt, dg) != (0, 0)]
-    peers = [sib, (pt, ph), (pt, pho), zup, zdn, xup, xdn]
-    peers += [at(dt, 2 * dg) for dt, dg in halo]
+    edge = 2 * c - 1
+    peers = [sib, (pt, ph), (pt, pho), zup, zdn, xup, xdn, at(-1, 0), at(1, 0)]
+    peers += [at(dt, edge) for dt in (-1, 0, 1)]
+
+    barrier = pltpu.get_barrier_semaphore()
+    for peer in peers:
+        pl.semaphore_signal(barrier, inc=1, device_id=peer, device_id_type=MESH)
 
     def rows(start, count):
         return pl.ds(pl.multiple_of(start, 16), count)
 
     own = rows(48 * h, 48)
+
+    def keep(col, values):
+        ga[own, pl.ds(col, values.shape[1])] = values
+
+    loads[0].wait()
     for part, col in ((1, K0), (2, V0), (0, Q0), (4, SO0), (3, CQ0), (5, CO0)):
         mine = pl.ds(pl.multiple_of(768 * part + HALF * c, 128), HALF)
         other = pl.ds(pl.multiple_of(768 * part + HALF * (1 - c), 128), HALF)
-        ga[own, pl.ds(col, HALF)] = w[:, mine]
         oth[:, pl.ds(col, HALF)] = w[:, other]
-
-    barrier = pltpu.get_barrier_semaphore()
-    for peer in peers:
-        pl.semaphore_signal(barrier, inc=1, device_id=peer, device_id_type=MESH)
+        if col in (K0, V0, SO0):
+            ga[own, pl.ds(col, HALF)] = w[:, mine]
+        else:
+            pl.when(lax.rem(h, 4) == x)(lambda col=col, mine=mine: keep(col, w[:, mine]))
     pl.semaphore_wait(barrier, len(peers))
 
     used = [0]
     started = []
 
-    def push(src, dst, peer, arriving):
-        i = used[0]
+    def index():
         used[0] += 1
-        copy = pltpu.make_async_remote_copy(
+        return used[0] - 1
+
+    def remote(src, dst, peer, i):
+        return pltpu.make_async_remote_copy(
             src_ref=src, dst_ref=dst, send_sem=send.at[i], recv_sem=recv.at[i],
             device_id=peer, device_id_type=MESH,
         )
+
+    def push(src, dst, peer, arriving):
+        i = index()
+        copy = remote(src, dst, peer, i)
         copy.start()
-        started.append(copy)
-        arrival = pltpu.make_async_remote_copy(
-            src_ref=arriving, dst_ref=arriving, send_sem=send.at[i], recv_sem=recv.at[i],
-            device_id=peer, device_id_type=MESH,
-        )
-        return arrival.wait_recv
+        started.append(copy.wait_send)
+        return remote(arriving, arriving, peer, i).wait_recv
 
     slab_waits = {}
 
@@ -100,6 +117,26 @@
             push(oth.at[:, cols], ga.at[own, cols], (pt, pho), ga.at[rows(48 * pho, 48), cols]),
         ]
 
+    def slab_one(lo, hi):
+        cols = pl.ds(lo, hi - lo)
+        piece = lax.rem(h, 4)
+        whole = ga.at[own, cols]
+        waits = []
+        for src, peer, row in (
+            (oth.at[:, cols], sib, hs),
+            (whole, (pt, ph), ph),
+            (oth.at[:, cols], (pt, pho), pho),
+        ):
+            copy = remote(src, whole, peer, index())
+            pl.when(piece == x)(copy.start)
+            started.append(lambda copy=copy: pl.when(piece == x)(copy.wait_send))
+            landed = ga.at[rows(48 * row, 48), cols]
+            arrival = remote(landed, landed, peer, used[0] - 1)
+            waits.append(
+                lambda arrival=arrival, row=row: pl.when(lax.rem(row, 4) == x)(arrival.wait_recv)
+            )
+        slab_waits[lo] = waits
+
     def slab_wait(lo):
         for wait in slab_waits[lo]:
             wait()
@@ -138,90 +175,110 @@
             return ga.at[rows(slot(step) + 48 * quarter, 48), cols]
 
         for s in range(4):
+            up = push(piece(-s, x), piece(-s, x), zup, piece(-s - 1, x))
+            dn = None
             if s < 3:
-                up = push(piece(-s, x), piece(-s, x), zup, piece(-s - 1, x))
                 dn = push(piece(s, x), piece(s, x), zdn, piece(s + 1, x))
-                yield
-                up()
+            yield
+            up()
+            if s < 3:
                 dn()
-            else:
-                up = push(piece(-s, x), piece(-s, x), zup, piece(-s - 1, x))
-                yield
-                up()
         left, right = lax.rem(x + 3, 4), lax.rem(x + 1, 4)
 
-        def fan(quarter, slabs, peer, count):
-            i = used[0]
-            used[0] += 1
+        def fan(quarter, slabs, peer):
+            i = index()
 
             def one(k, carry):
                 part = piece(k, quarter)
-                pltpu.make_async_remote_copy(
-                    src_ref=part, dst_ref=part, send_sem=send.at[i], recv_sem=recv.at[i],
-                    device_id=peer, device_id_type=MESH,
-                ).start()
+                remote(part, part, peer, i).start()
                 return carry
 
             lax.fori_loop(slabs[0], slabs[1], one, 0)
-            whole = ga.at[pl.ds(0, 48 * count), cols]
-            copy = pltpu.make_async_remote_copy(
-                src_ref=whole, dst_ref=whole, send_sem=send.at[i], recv_sem=recv.at[i],
-                device_id=peer, device_id_type=MESH,
-            )
-            started.append(copy)
+            whole = ga.at[pl.ds(0, 48 * (slabs[1] - slabs[0])), cols]
+            copy = remote(whole, whole, peer, i)
+            started.append(copy.wait_send)
             return copy.wait_recv
 
-        to_up = fan(x, (1, 8), xup, 7)
-        to_dn = fan(x, (1, 8), xdn, 7)
+        to_up = fan(x, (0, 8), xup)
+        to_dn = fan(x, (0, 8), xdn)
         yield
         to_up()
         to_dn()
-        to_up = fan(left, (1, 5), xup, 4)
-        to_dn = fan(right, (5, 8), xdn, 3)
+        to_up = fan(left, (0, 4), xup)
+        to_dn = fan(right, (4, 8), xdn)
         yield
         to_up()
         to_dn()
         yield from finish(lo, hi, forward)
 
-    chunks = ((K0, V0), (V0, Q0), (Q0, SO0), (SO0, CQ0))
-    for lo, hi in chunks:
-        slab(lo, hi)
-
-    ring_k, ring_v = ring_z(K0, V0, False), ring_z(V0, Q0, False)
-    ring_q, ring_so = ring_x(Q0, SO0, False), ring_z(SO0, CQ0, True)
-    ring_cq, ring_co = ring_x(CQ0, CO0, True), ring_x(CO0, END, True)
-
-    def pump(*rings):
-        for ring in rings:
-            next(ring, None)
-
-    def drain(*rings):
-        for ring in rings:
-            for _ in ring:
+    def send_latent():
+        waits = []
+        for place, dt, dh in ((1, -1, 0), (0, 1, 0), (4, -1, edge), (3, 0, edge), (2, 1, edge)):
+            waits.append((place, push(lat_in, lats.at[place], at(dt, dh), lats.at[place])))
+        return dict(waits)
+
+    slab(K0, V0)
+    slab(V0, Q0)
+    slab_one(Q0, SO0)
+    slab(SO0, CQ0)
+    got_latent = send_latent()
+
+    rings = {
+        "k": ring_z(K0, V0, False),
+        "v": ring_z(V0, Q0, False),
+        "q": ring_x(Q0, SO0, False),
+        "so": ring_z(SO0, CQ0, True),
+        "cq": ring_x(CQ0, CO0, True),
+        "co": ring_x(CO0, END, True),
+    }
+
+    def pump(*names):
+        for name in names:
+            next(rings[name], None)
+
+    def drain(*names):
+        for name in names:
+            for _ in rings[name]:
                 pass
 
-    pump(ring_k, ring_v, ring_q)
-
-    mine = rows(TOK * c, TOK)
-    theirs = rows(TOK * (1 - c), TOK)
-    latent = lat[...].astype(F32)
-    modb[mine, :] = (layer_norm(latent) * (1.0 + mod[1:2, :]) + mod[0:1, :]).astype(BF)
-    got_mod = push(modb.at[mine, :], modb.at[mine, :], sib, modb.at[theirs, :])
-
+    pump("k", "v", "q")
+
+    shown = [(0, 1 + c), (2, 1 + c), (0, 3 * c), (1, 3 * c), (2, 3 * c), (1, 1 + c)]
+    hidden = [(0, 2 - c), (2, 2 - c), (0, 3 - 3 * c), (1, 3 - 3 * c), (2, 3 - 3 * c), (1, 2 - c)]
+    got_mod = {}
+
+    def modulate(place, src):
+        f, r = shown[place]
+        here = modb.at[f, rows(TOK * r, TOK)]
+        values = layer_norm(src[...].astype(F32)) * (1.0 + mod[1:2, :]) + mod[0:1, :]
+        here[...] = values.astype(BF)
+        f, r = hidden[place]
+        got_mod[place] = push(here, here, sib, modb.at[f, rows(TOK * r, TOK)])
+
+    def modulate_halo(place):
+        got_latent[place]()
+        modulate(place, lats.at[place])
+
+    loads[1].wait()
+    modulate(5, lat)
+
+    loads[2].wait()
+    loads[3].wait()
     txt[...] = dot_nt(wt[...], ts[...]).astype(BF)
-    ga[own, pl.ds(TX0, 256)] = txt[:, pl.ds(pl.multiple_of(256 * c, 128), 256)]
+    mine = pl.ds(pl.multiple_of(256 * c, 128), 256)
+    pl.when(lax.rem(h, 4) == x)(lambda mine=mine: keep(TX0, txt[:, mine]))
     oth[:, pl.ds(TX0, 256)] = txt[:, pl.ds(pl.multiple_of(256 * (1 - c), 128), 256)]
-    slab(CQ0, CO0)
-    slab(CO0, END)
-    pump(ring_k, ring_v, ring_q)
+    slab_one(CQ0, CO0)
+    slab_one(CO0, END)
+    pump("k", "v", "q")
 
     lane = lax.broadcasted_iota(jnp.int32, (8, WIN), 1)
     frame = lax.broadcasted_iota(jnp.int32, (8, WIN), 0)
 
     def step_of(value, *edges):
         total = jnp.zeros_like(value)
-        for edge in edges:
-            total = total + (value >= edge).astype(jnp.int32)
+        for mark_at in edges:
+            total = total + (value >= mark_at).astype(jnp.int32)
         return total
 
     row_at = step_of(lane, 208, 416)
@@ -238,7 +295,6 @@
             allowed = allowed | (code == target)
         rb[c, pl.ds(8 * q, 8), :] = jnp.where(allowed, 0.0, -jnp.inf).astype(F32)
     got_rb = push(rb.at[c], rb.at[c], sib, rb.at[1 - c])
-    pump(ring_k, ring_v, ring_q)
     got_rb()
     token = lax.broadcasted_iota(jnp.int32, (TOK, 1), 0)
     token = token - 104 * step_of(token, 104)
@@ -255,56 +311,79 @@
     lax.fori_loop(0, 6, masks, 0)
     for f in range(3):
         kvb[f, pl.ds(832, 16), :] = jnp.zeros((16, 768), BF)
-    pump(ring_k, ring_v, ring_q)
-    got_mod()
-    drain(ring_k, ring_v)
-    pump(ring_so, ring_cq, ring_co)
-
-    both = pl.ds(TOK, 2 * TOK)
-    raw[...] = dot(modb[...], ga[:, pl.ds(K0, HALF)])
-
-    def squares(i):
-        ssb[i, 0] = jnp.broadcast_to(
-            jnp.sum(raw[...] * raw[...], axis=-1, keepdims=True), (2 * TOK, 128)
-        )
-        return push(ssb.at[i, 0], ssb.at[i, 1], sib, ssb.at[i, 1])
+    pump("k", "v", "q")
 
     def gain(i, half):
         return ng[i : i + 1, pl.ds(pl.multiple_of(HALF * half, 128), HALF)]
 
-    def normal(i, gains):
-        total = ssb[i, 0, :, 0:1] + ssb[i, 1, :, 0:1]
-        return raw[...] * lax.rsqrt(total * (1.0 / 768) + 1e-06) * gains
-
-    def send_halo(lo):
-        cols = pl.ds(lo, HALF)
-        waits = []
-        for dt, dg in halo:
-            first, count = (TOK, 2 * TOK) if dg == 0 else (2 * TOK, TOK) if dg > 0 else (TOK, TOK)
-            there = TOK if dg == 0 else 0 if dg > 0 else 3 * TOK
-            src = kvb.at[1, pl.ds(first, count), cols]
-            dst = kvb.at[1 - dt, pl.ds(there, count), cols]
-            waits.append(push(src, dst, at(dt, 2 * dg), dst))
-        return waits
-
-    got_k_squares = squares(0)
-    kvb[1, both, pl.ds(HALF, HALF)] = dot(modb[...], ga[:, pl.ds(V0, HALF)]).astype(BF)
-    v_waits = send_halo(HALF)
-    got_k_squares()
-    kvb[1, both, pl.ds(0, HALF)] = normal(0, gain(1, c)).astype(BF)
-    k_waits = send_halo(0)
-
-    drain(ring_q)
-    pump(ring_so, ring_cq, ring_co)
-    raw[...] = dot(modb[...], ga[:, pl.ds(Q0, HALF)])
-    got_q_squares = squares(1)
-    pump(ring_so, ring_cq, ring_co)
-    got_q_squares()
-    qb[...] = normal(1, gain(0, c) * SCALE).astype(BF)
-    for _ in range(4):
-        pump(ring_so, ring_cq, ring_co)
-    for wait in v_waits + k_waits:
-        wait()
+    def squares(values, mine_at, theirs_at):
+        total = jnp.sum(values * values, axis=-1, keepdims=True)
+        mine_at[...] = jnp.broadcast_to(total, mine_at.shape)
+        return push(mine_at, theirs_at, sib, theirs_at)
+
+    def inverse_rms(mine_at, theirs_at):
+        total = mine_at[:, 0:1] + theirs_at[:, 0:1]
+        return lax.rsqrt(total * (1.0 / 768) + 1e-06)
+
+    got_squares = {}
+
+    def keys_values(f, r, n):
+        here, flat = pl.ds(TOK * r, TOK * n), pl.ds(TOK * (4 * f + r), TOK * n)
+        modulated = modb[f, here, :]
+        keys = dot(modulated, ga[:, pl.ds(K0, HALF)])
+        kraw[flat, :] = keys
+        got_squares[f, r, n] = squares(keys, ssb.at[0, flat], ssb.at[1, flat])
+        kvb[f, here, pl.ds(HALF, HALF)] = dot(modulated, ga[:, pl.ds(V0, HALF)]).astype(BF)
+
+    def normal_keys(f, r, n):
+        here, flat = pl.ds(TOK * r, TOK * n), pl.ds(TOK * (4 * f + r), TOK * n)
+        got_squares[f, r, n]()
+        scaled = kraw[flat, :] * inverse_rms(ssb.at[0, flat], ssb.at[1, flat])
+        kvb[f, here, pl.ds(0, HALF)] = (scaled * gain(1, c)).astype(BF)
+
+    both = pl.ds(TOK, 2 * TOK)
+    got_queries = []
+
+    def queries():
+        raw[...] = dot(modb[1, both, :], ga[:, pl.ds(Q0, HALF)])
+        got_queries.append(squares(raw[...], ssq.at[0], ssq.at[1]))
+
+    def normal_queries():
+        got_queries[0]()
+        qb[...] = (raw[...] * inverse_rms(ssq.at[0], ssq.at[1]) * (gain(0, c) * SCALE)).astype(BF)
+
+    pump("k", "v", "q")
+    modulate_halo(0)
+    modulate_halo(1)
+    drain("k", "v")
+    pump("so", "cq", "co", "q")
+    got_mod[5]()
+    keys_values(1, 1, 2)
+    pump("cq", "co", "so")
+    got_mod[0]()
+    keys_values(0, 1, 2)
+    normal_keys(1, 1, 2)
+    got_mod[1]()
+    keys_values(2, 1, 2)
+    normal_keys(0, 1, 2)
+    pump("cq", "co", "so", "q")
+    normal_keys(2, 1, 2)
+    pump("cq", "co", "so")
+    drain("q")
+    queries()
+    pump("cq", "co", "so")
+    for place in (2, 3, 4):
+        modulate_halo(place)
+    normal_queries()
+    for f in range(3):
+        got_mod[2 + f]()
+        keys_values(f, 0, 1)
+        keys_values(f, 3, 1)
+        if f == 0:
+            pump("cq", "co", "so")
+    for f in range(3):
+        normal_keys(f, 0, 1)
+        normal_keys(f, 3, 1)
 
     def attend(r, i):
         q = qb[pl.ds(TOK * r, TOK), pl.ds(128 * i, 128)]
@@ -323,9 +402,11 @@
     for r in range(2):
         for i in range(3):
             attend(r, i)
-            pump(ring_so, ring_cq, ring_co)
+            pump("cq", "co", "so")
+    mine = rows(TOK * c, TOK)
+    theirs = rows(TOK * (1 - c), TOK)
     got_mix = push(mixb.at[theirs, :], mixo, sib, mixo)
-    drain(ring_so)
+    drain("so")
     got_mix()
 
     def outward(mine_in, other_in, lo, i):
@@ -342,7 +423,7 @@
         return carry
 
     lax.fori_loop(0, 6, self_out, 0)
-    drain(ring_cq)
+    drain("cq")
     normed = (layer_norm(res[...]) * cn[0:1, :] + cn[1:2, :]).astype(BF)
     cq_mine = dot(normed, ga[:, pl.ds(CQ0, HALF)])
     cq_other = dot(normed, gb[:, pl.ds(CQ0 - SO0, HALF)])
@@ -356,7 +437,9 @@
         keys = ref[0:768, pl.ds(lo, 256)].astype(F32)
         return lax.rsqrt(jnp.sum(keys * keys, axis=0, keepdims=True) * (1.0 / 768) + 1e-06)
 
-    real = [tmask[pl.ds(c, 1), :] == 1, tmask[pl.ds(1 - c, 1), :] == 1]
+    real = [
+        tmask[:, pl.ds(pl.multiple_of(256 * half, 128), 256)] == 1 for half in (c, 1 - c)
+    ]
     parts = [(ga, TX0), (gb, TX0 - SO0)]
     scales = [text_scale(*part) for part in parts]
     for k in range(2):
@@ -378,7 +461,7 @@
                 total = total + jnp.sum(p, axis=-1, keepdims=True)
                 mixed = mixed + dot_nt(p.astype(BF), ref[vrow, pl.ds(lo, 256)])
             qb[pl.ds(TOK * k, TOK), pl.ds(128 * i, 128)] = (mixed / total).astype(BF)
-    drain(ring_co)
+    drain("co")
     cross_mine, cross_other = qb[0:TOK, :], qb[TOK : 2 * TOK, :]
 
     def cross_out(i, carry):
@@ -387,8 +470,9 @@
         return carry
 
     lax.fori_loop(0, 6, cross_out, 0)
-    for copy in started:
-        copy.wait_send()
+    assert used[0] <= NSEM
+    for wait in started:
+        wait()
 
 
 def body(
@@ -396,19 +480,27 @@
 ):
     vmem = pl.BlockSpec(memory_space=pltpu.VMEM)
     smem = pl.BlockSpec(memory_space=pltpu.SMEM)
+    hbm = pl.BlockSpec(memory_space=pl.ANY)
     result = pl.pallas_call(
         kernel,
         out_shape=jax.ShapeDtypeStruct((TOK, D), BF),
-        in_specs=[vmem] * 7 + [smem, vmem],
+        in_specs=[hbm, vmem, vmem, vmem, hbm, hbm, hbm, smem, vmem],
         out_specs=vmem,
         scratch_shapes=[
+            pltpu.VMEM((TOK, D), BF),
+            pltpu.VMEM((48, 4608), BF),
+            pltpu.VMEM((512, D), BF),
+            pltpu.VMEM((48, D), BF),
             pltpu.VMEM((D, END), BF),
             pltpu.VMEM((D, END - SO0), BF),
             pltpu.VMEM((48, END), BF),
-            pltpu.VMEM((2 * TOK, D), BF),
+            pltpu.VMEM((3, 4 * TOK, D), BF),
+            pltpu.VMEM((5, TOK, D), BF),
             pltpu.VMEM((3, 848, 768), BF),
+            pltpu.VMEM((12 * TOK, HALF), F32),
+            pltpu.VMEM((2, 12 * TOK, 128), F32),
             pltpu.VMEM((2 * TOK, HALF), F32),
-            pltpu.VMEM((2, 2, 2 * TOK, 128), F32),
+            pltpu.VMEM((2, 2 * TOK, 128), F32),
             pltpu.VMEM((2 * TOK, HALF), BF),
             pltpu.VMEM((2, 32, WIN), F32),
             pltpu.VMEM((2, 3, TOK, WIN), F32),
@@ -418,6 +510,7 @@
             pltpu.VMEM((48, 512), BF),
             pltpu.SemaphoreType.DMA((NSEM,)),
             pltpu.SemaphoreType.DMA((NSEM,)),
+            pltpu.SemaphoreType.DMA((4,)),
         ],
         compiler_params=pltpu.CompilerParams(
             collective_id=0, has_side_effects=True, vmem_limit_bytes=60 * 1024 * 1024
@@ -434,7 +527,7 @@
         text_states,
         w_text.T,
         tile_offsets,
-        text_mask.reshape(2, 256),
+        text_mask.reshape(1, 512),
     )
     return result.reshape(latent.shape)
 

time: 153 us -> 138 us (0.902); the launches traced: 150 us -> 138 us
  Pallas kernels: 147 us -> 136 us
    pallas_call x1, Pallas kernels: 147 us -> 136 us  [body(): pl.pallas_call(kernel, out_shape=jax.ShapeDtypeStruct((TOK, D), BF), in_s...]
where the time goes in v2:
time: 138 us
  Pallas kernels  136 us (99%)
  local copies, waits for them, and re-layouts  1.95 us (1%)
    pallas_call x1, Pallas kernels, body(): pl.pallas_call(kernel, out_shape=jax.ShapeDtypeStruct((TOK, D), BF), in_s...  136 us

profile of v2, /device:TPU:1, one launch (start us, length us, event | category | flops | bytes accessed | tf_op | source)
XLA Modules:
  0.0 138.1 jit_solution(14155919963835135458)
XLA Ops:
  0.0 136.1 %shard_map.91 = bf16[208,1536]{1,0:T(8,128)(2,1)} custom-call(bf16[208,1536]{1,0:T(8,128)(2,1)} %bitcast.5, f32[3,1536]{1,0:T(4,128)} %mod.1, f32[2,1536]{1,0:T(2,128)} %cn.1, f32[4,768]{1,0:T(4,128)} %ng.1, bf16[48,4608]{1,0:T(8,128)(2,1)} %w_in.1, bf16[512,1536]{1,0:T(8,128)(2,1)} %ts_in.1, bf16[48,1536]{1,0:T(8,128)(2,1)} %bitcast.6, ...), custom_call_target="tpu_custom_call" | custom-call | flops 6000000000 | bytes 6000000 | tf_op jit(solution)/shard_map/pallas_call | solution.py:484
  136.1 2.0 %copy.11 = bf16[1,2,104,1536]{3,2,1,0:T(8,128)(2,1)} copy(bf16[1,2,104,1536]{3,2,1,0:T(8,128)(2,1)} %bitcast.4) | data formatting | bytes 1277952

commit v3 on v2

--- a/solution.py
+++ b/solution.py
@@ -61,8 +61,8 @@
     pho = ph + 1 - 2 * c
     zup, zdn, xup, xdn = at(0, 4), at(0, -4), at(2, 0), at(-2, 0)
     edge = 2 * c - 1
-    peers = [sib, (pt, ph), (pt, pho), zup, zdn, xup, xdn, at(-1, 0), at(1, 0)]
-    peers += [at(dt, edge) for dt in (-1, 0, 1)]
+    flip, outer, beyond = at(1 - 2 * ylo, 0), at(2 * ylo - 1, 0), at(2 - 4 * ylo, 0)
+    peers = [sib, (pt, ph), (pt, pho), zup, zdn, xup, xdn, flip, outer, at(0, edge)]
 
     barrier = pltpu.get_barrier_semaphore()
     for peer in peers:
@@ -174,6 +174,21 @@
         def piece(step, quarter):
             return ga.at[rows(slot(step) + 48 * quarter, 48), cols]
 
+        fan_up, fan_dn = index(), index()
+
+        def spread(*steps):
+            for step in steps:
+                part = piece(step, x)
+                remote(part, part, xup, fan_up).start()
+                remote(part, part, xdn, fan_dn).start()
+
+        def gathered(peer, i, count):
+            whole = ga.at[pl.ds(0, 48 * count), cols]
+            copy = remote(whole, whole, peer, i)
+            started.append(copy.wait_send)
+            return copy.wait_recv
+
+        spread(0)
         for s in range(4):
             up = push(piece(-s, x), piece(-s, x), zup, piece(-s - 1, x))
             dn = None
@@ -183,6 +198,11 @@
             up()
             if s < 3:
                 dn()
+                spread(-s - 1, s + 1)
+            else:
+                spread(-s - 1)
+        to_up = gathered(xup, fan_up, 8)
+        to_dn = gathered(xdn, fan_dn, 8)
         left, right = lax.rem(x + 3, 4), lax.rem(x + 1, 4)
 
         def fan(quarter, slabs, peer):
@@ -194,13 +214,8 @@
                 return carry
 
             lax.fori_loop(slabs[0], slabs[1], one, 0)
-            whole = ga.at[pl.ds(0, 48 * (slabs[1] - slabs[0])), cols]
-            copy = remote(whole, whole, peer, i)
-            started.append(copy.wait_send)
-            return copy.wait_recv
-
-        to_up = fan(x, (0, 8), xup)
-        to_dn = fan(x, (0, 8), xdn)
+            return gathered(peer, i, slabs[1] - slabs[0])
+
         yield
         to_up()
         to_dn()
@@ -211,17 +226,16 @@
         to_dn()
         yield from finish(lo, hi, forward)
 
-    def send_latent():
-        waits = []
-        for place, dt, dh in ((1, -1, 0), (0, 1, 0), (4, -1, edge), (3, 0, edge), (2, 1, edge)):
-            waits.append((place, push(lat_in, lats.at[place], at(dt, dh), lats.at[place])))
-        return dict(waits)
-
+    def send_latent(place, src, peer):
+        got_latent[place] = push(src, lats.at[place], peer, lats.at[place])
+
+    got_latent = {}
     slab(K0, V0)
+    slab_one(Q0, SO0)
+    slab_one(CO0, END)
     slab(V0, Q0)
-    slab_one(Q0, SO0)
-    slab(SO0, CQ0)
-    got_latent = send_latent()
+    send_latent(0, lat_in, flip)
+    send_latent(3, lat_in, at(0, edge))
 
     rings = {
         "k": ring_z(K0, V0, False),
@@ -241,10 +255,12 @@
             for _ in rings[name]:
                 pass
 
-    pump("k", "v", "q")
-
-    shown = [(0, 1 + c), (2, 1 + c), (0, 3 * c), (1, 3 * c), (2, 3 * c), (1, 1 + c)]
-    hidden = [(0, 2 - c), (2, 2 - c), (0, 3 - 3 * c), (1, 3 - 3 * c), (2, 3 - 3 * c), (1, 2 - c)]
+    pump("k", "q", "co", "v")
+
+    near, far = 2 - 2 * ylo, 2 * ylo
+    places = [(near, 1), (far, 1), (near, 0), (1, 0), (far, 0), (1, 1)]
+    shown = [(f, 1 + c if own_row else 3 * c) for f, own_row in places]
+    hidden = [(f, 2 - c if own_row else 3 - 3 * c) for f, own_row in places]
     got_mod = {}
 
     def modulate(place, src):
@@ -256,7 +272,6 @@
         got_mod[place] = push(here, here, sib, modb.at[f, rows(TOK * r, TOK)])
 
     def modulate_halo(place):
-        got_latent[place]()
         modulate(place, lats.at[place])
 
     loads[1].wait()
@@ -269,8 +284,8 @@
     pl.when(lax.rem(h, 4) == x)(lambda mine=mine: keep(TX0, txt[:, mine]))
     oth[:, pl.ds(TX0, 256)] = txt[:, pl.ds(pl.multiple_of(256 * (1 - c), 128), 256)]
     slab_one(CQ0, CO0)
-    slab_one(CO0, END)
-    pump("k", "v", "q")
+    pump("cq")
+    pump("k", "q", "co", "v")
 
     lane = lax.broadcasted_iota(jnp.int32, (8, WIN), 1)
     frame = lax.broadcasted_iota(jnp.int32, (8, WIN), 0)
@@ -311,7 +326,10 @@
     lax.fori_loop(0, 6, masks, 0)
     for f in range(3):
         kvb[f, pl.ds(832, 16), :] = jnp.zeros((16, 768), BF)
-    pump("k", "v", "q")
+    pump("cq")
+    got_latent[0]()
+    send_latent(1, lats.at[0], beyond)
+    pump("k", "q", "co", "v", "cq")
 
     def gain(i, half):
         return ng[i : i + 1, pl.ds(pl.multiple_of(HALF * half, 128), HALF)]
@@ -327,17 +345,17 @@
 
     got_squares = {}
 
-    def keys_values(f, r, n):
-        here, flat = pl.ds(TOK * r, TOK * n), pl.ds(TOK * (4 * f + r), TOK * n)
+    def keys_values(name, f, r, n):
+        here, flat = pl.ds(TOK * r, TOK * n), rows(TOK * (4 * f + r), TOK * n)
         modulated = modb[f, here, :]
         keys = dot(modulated, ga[:, pl.ds(K0, HALF)])
         kraw[flat, :] = keys
-        got_squares[f, r, n] = squares(keys, ssb.at[0, flat], ssb.at[1, flat])
+        got_squares[name] = squares(keys, ssb.at[0, flat], ssb.at[1, flat])
         kvb[f, here, pl.ds(HALF, HALF)] = dot(modulated, ga[:, pl.ds(V0, HALF)]).astype(BF)
 
-    def normal_keys(f, r, n):
-        here, flat = pl.ds(TOK * r, TOK * n), pl.ds(TOK * (4 * f + r), TOK * n)
-        got_squares[f, r, n]()
+    def normal_keys(name, f, r, n):
+        here, flat = pl.ds(TOK * r, TOK * n), rows(TOK * (4 * f + r), TOK * n)
+        got_squares[name]()
         scaled = kraw[flat, :] * inverse_rms(ssb.at[0, flat], ssb.at[1, flat])
         kvb[f, here, pl.ds(0, HALF)] = (scaled * gain(1, c)).astype(BF)
 
@@ -352,38 +370,53 @@
         got_queries[0]()
         qb[...] = (raw[...] * inverse_rms(ssq.at[0], ssq.at[1]) * (gain(0, c) * SCALE)).astype(BF)
 
-    pump("k", "v", "q")
     modulate_halo(0)
+    got_latent[3]()
+    send_latent(2, lats.at[3], flip)
+    send_latent(4, lats.at[3], outer)
+    pump("k", "q", "co", "v", "cq")
+    slab(SO0, CQ0)
+    modulate_halo(3)
+    drain("k", "v")
+    pump("so", "q", "co", "cq")
+    got_mod[5]()
+    keys_values("own", 1, 1, 2)
+    pump("so")
+    got_mod[0]()
+    keys_values("near", near, 1, 2)
+    normal_keys("own", 1, 1, 2)
+    pump("q", "co", "cq")
+    got_latent[1]()
     modulate_halo(1)
-    drain("k", "v")
-    pump("so", "cq", "co", "q")
-    got_mod[5]()
-    keys_values(1, 1, 2)
-    pump("cq", "co", "so")
-    got_mod[0]()
-    keys_values(0, 1, 2)
-    normal_keys(1, 1, 2)
-    got_mod[1]()
-    keys_values(2, 1, 2)
-    normal_keys(0, 1, 2)
-    pump("cq", "co", "so", "q")
-    normal_keys(2, 1, 2)
-    pump("cq", "co", "so")
+    normal_keys("near", near, 1, 2)
     drain("q")
     queries()
-    pump("cq", "co", "so")
-    for place in (2, 3, 4):
-        modulate_halo(place)
+    pump("so", "co", "cq")
+    got_mod[3]()
+    keys_values("edge0", 1, 0, 1)
+    keys_values("edge3", 1, 3, 1)
     normal_queries()
-    for f in range(3):
-        got_mod[2 + f]()
-        keys_values(f, 0, 1)
-        keys_values(f, 3, 1)
-        if f == 0:
-            pump("cq", "co", "so")
-    for f in range(3):
-        normal_keys(f, 0, 1)
-        normal_keys(f, 3, 1)
+    got_mod[1]()
+    keys_values("far", far, 1, 2)
+    normal_keys("edge0", 1, 0, 1)
+    normal_keys("edge3", 1, 3, 1)
+    pump("so", "co", "cq")
+    got_latent[2]()
+    modulate_halo(2)
+    normal_keys("far", far, 1, 2)
+    got_latent[4]()
+    modulate_halo(4)
+    got_mod[2]()
+    keys_values("near0", near, 0, 1)
+    keys_values("near3", near, 3, 1)
+    got_mod[4]()
+    keys_values("far0", far, 0, 1)
+    keys_values("far3", far, 3, 1)
+    normal_keys("near0", near, 0, 1)
+    normal_keys("near3", near, 3, 1)
+    pump("so")
+    normal_keys("far0", far, 0, 1)
+    normal_keys("far3", far, 3, 1)
 
     def attend(r, i):
         q = qb[pl.ds(TOK * r, TOK), pl.ds(128 * i, 128)]

time: 138 us -> 110 us (0.80)
  Pallas kernels: 136 us -> 108 us
    pallas_call x1, Pallas kernels: 136 us -> 108 us  [body(): pl.pallas_call(kernel, out_shape=jax.ShapeDtypeStruct((TOK, D), BF), in_s...]
where the time goes in v3:
time: 110 us
  Pallas kernels  108 us (98%)
  local copies, waits for them, and re-layouts  1.95 us (2%)
    pallas_call x1, Pallas kernels, body(): pl.pallas_call(kernel, out_shape=jax.ShapeDtypeStruct((TOK, D), BF), in_s...  108 us

profile of v3, /device:TPU:1, one launch (start us, length us, event | category | flops | bytes accessed | tf_op | source)
XLA Modules:
  0.0 109.6 jit_solution(17806714771670933609)
XLA Ops:
  0.0 107.7 %shard_map.91 = bf16[208,1536]{1,0:T(8,128)(2,1)} custom-call(bf16[208,1536]{1,0:T(8,128)(2,1)} %bitcast.5, f32[3,1536]{1,0:T(4,128)} %mod.1, f32[2,1536]{1,0:T(2,128)} %cn.1, f32[4,768]{1,0:T(4,128)} %ng.1, bf16[48,4608]{1,0:T(8,128)(2,1)} %w_in.1, bf16[512,1536]{1,0:T(8,128)(2,1)} %ts_in.1, bf16[48,1536]{1,0:T(8,128)(2,1)} %bitcast.6, ...), custom_call_target="tpu_custom_call" | custom-call | flops 6000000000 | bytes 6000000 | tf_op jit(solution)/shard_map/pallas_call | solution.py:517
  107.7 2.0 %copy.11 = bf16[1,2,104,1536]{3,2,1,0:T(8,128)(2,1)} copy(bf16[1,2,104,1536]{3,2,1,0:T(8,128)(2,1)} %bitcast.4) | data formatting | bytes 1277952

commit v4 on v3

--- a/solution.py
+++ b/solution.py
@@ -15,6 +15,7 @@
 SCALE = 128.0**-0.5 * 1.4426950408889634
 K0, V0, Q0, SO0, CQ0, TX0, CO0, END = 0, 384, 768, 1152, 1536, 1920, 2176, 2560
 NSEM = 160
+LAG = 0
 
 
 def layer_norm(values):
@@ -81,7 +82,7 @@
         mine = pl.ds(pl.multiple_of(768 * part + HALF * c, 128), HALF)
         other = pl.ds(pl.multiple_of(768 * part + HALF * (1 - c), 128), HALF)
         oth[:, pl.ds(col, HALF)] = w[:, other]
-        if col in (K0, V0, SO0):
+        if col in (K0, V0, SO0, CO0):
             ga[own, pl.ds(col, HALF)] = w[:, mine]
         else:
             pl.when(lax.rem(h, 4) == x)(lambda col=col, mine=mine: keep(col, w[:, mine]))
@@ -174,13 +175,8 @@
         def piece(step, quarter):
             return ga.at[rows(slot(step) + 48 * quarter, 48), cols]
 
-        fan_up, fan_dn = index(), index()
-
-        def spread(*steps):
-            for step in steps:
-                part = piece(step, x)
-                remote(part, part, xup, fan_up).start()
-                remote(part, part, xdn, fan_dn).start()
+        left, right = lax.rem(x + 3, 4), lax.rem(x + 1, 4)
+        last_up, last_dn = index(), index()
 
         def gathered(peer, i, count):
             whole = ga.at[pl.ds(0, 48 * count), cols]
@@ -188,39 +184,46 @@
             started.append(copy.wait_send)
             return copy.wait_recv
 
-        spread(0)
-        for s in range(4):
-            up = push(piece(-s, x), piece(-s, x), zup, piece(-s - 1, x))
-            dn = None
+        def beside(*steps):
+            i, j = index(), index()
+            for step in steps:
+                part = piece(step, x)
+                remote(part, part, xup, i).start()
+                remote(part, part, xdn, j).start()
+            return steps, gathered(xup, i, len(steps)), gathered(xdn, j, len(steps))
+
+        def pass_on(steps, from_left, from_right):
+            from_left()
+            from_right()
+            if steps[0] != -4:
+                part = piece(steps[0], left)
+                remote(part, part, xup, last_up).start()
+            if steps[-1] != 0:
+                part = piece(steps[-1], right)
+                remote(part, part, xdn, last_dn).start()
+
+        def along(s):
+            waits = [push(piece(-s, x), piece(-s, x), zup, piece(-s - 1, x))]
             if s < 3:
-                dn = push(piece(s, x), piece(s, x), zdn, piece(s + 1, x))
+                waits.append(push(piece(s, x), piece(s, x), zdn, piece(s + 1, x)))
+            return waits
+
+        waits, held = along(0), [beside(0)]
+        for s in range(1, 5):
             yield
-            up()
-            if s < 3:
-                dn()
-                spread(-s - 1, s + 1)
+            for wait in waits:
+                wait()
+            if s < 4:
+                waits = along(s)
+                held.append(beside(-s, s))
             else:
-                spread(-s - 1)
-        to_up = gathered(xup, fan_up, 8)
-        to_dn = gathered(xdn, fan_dn, 8)
-        left, right = lax.rem(x + 3, 4), lax.rem(x + 1, 4)
-
-        def fan(quarter, slabs, peer):
-            i = index()
-
-            def one(k, carry):
-                part = piece(k, quarter)
-                remote(part, part, peer, i).start()
-                return carry
-
-            lax.fori_loop(slabs[0], slabs[1], one, 0)
-            return gathered(peer, i, slabs[1] - slabs[0])
-
-        yield
-        to_up()
-        to_dn()
-        to_up = fan(left, (0, 4), xup)
-        to_dn = fan(right, (4, 8), xdn)
+                held.append(beside(-s))
+            if s > LAG:
+                pass_on(*held.pop(0))
+        while held:
+            yield
+            pass_on(*held.pop(0))
+        to_up, to_dn = gathered(xup, last_up, 4), gathered(xdn, last_dn, 4)
         yield
         to_up()
         to_dn()
@@ -232,10 +235,9 @@
     got_latent = {}
     slab(K0, V0)
     slab_one(Q0, SO0)
-    slab_one(CO0, END)
     slab(V0, Q0)
     send_latent(0, lat_in, flip)
-    send_latent(3, lat_in, at(0, edge))
+    slab(SO0, CQ0)
 
     rings = {
         "k": ring_z(K0, V0, False),
@@ -243,7 +245,7 @@
         "q": ring_x(Q0, SO0, False),
         "so": ring_z(SO0, CQ0, True),
         "cq": ring_x(CQ0, CO0, True),
-        "co": ring_x(CO0, END, True),
+        "co": ring_z(CO0, END, True),
     }
 
     def pump(*names):
@@ -255,7 +257,7 @@
             for _ in rings[name]:
                 pass
 
-    pump("k", "q", "co", "v")
+    pump("q", "k", "v")
 
     near, far = 2 - 2 * ylo, 2 * ylo
     places = [(near, 1), (far, 1), (near, 0), (1, 0), (far, 0), (1, 1)]
@@ -284,8 +286,9 @@
     pl.when(lax.rem(h, 4) == x)(lambda mine=mine: keep(TX0, txt[:, mine]))
     oth[:, pl.ds(TX0, 256)] = txt[:, pl.ds(pl.multiple_of(256 * (1 - c), 128), 256)]
     slab_one(CQ0, CO0)
+    slab(CO0, END)
     pump("cq")
-    pump("k", "q", "co", "v")
+    send_latent(3, lat_in, at(0, edge))
 
     lane = lax.broadcasted_iota(jnp.int32, (8, WIN), 1)
     frame = lax.broadcasted_iota(jnp.int32, (8, WIN), 0)
@@ -326,10 +329,10 @@
     lax.fori_loop(0, 6, masks, 0)
     for f in range(3):
         kvb[f, pl.ds(832, 16), :] = jnp.zeros((16, 768), BF)
-    pump("cq")
+    pump("k", "q", "v", "cq")
     got_latent[0]()
     send_latent(1, lats.at[0], beyond)
-    pump("k", "q", "co", "v", "cq")
+    pump("k", "q", "v", "cq")
 
     def gain(i, half):
         return ng[i : i + 1, pl.ds(pl.multiple_of(HALF * half, 128), HALF)]
@@ -374,8 +377,7 @@
     got_latent[3]()
     send_latent(2, lats.at[3], flip)
     send_latent(4, lats.at[3], outer)
-    pump("k", "q", "co", "v", "cq")
-    slab(SO0, CQ0)
+    pump("k", "q", "v", "cq")
     modulate_halo(3)
     drain("k", "v")
     pump("so", "q", "co", "cq")

time: 110 us -> 109 us (level)
  no operation moved by 1% of the time
where the time goes in v4:
time: 109 us
  Pallas kernels  107 us (98%)
  local copies, waits for them, and re-layouts  1.95 us (2%)
    pallas_call x1, Pallas kernels, body(): pl.pallas_call(kernel, out_shape=jax.ShapeDtypeStruct((TOK, D), BF), in_s...  107 us

profile of v4, /device:TPU:1, one launch (start us, length us, event | category | flops | bytes accessed | tf_op | source)
XLA Modules:
  0.0 108.8 jit_solution(16031238681164755909)
XLA Ops:
  0.0 106.8 %shard_map.91 = bf16[208,1536]{1,0:T(8,128)(2,1)} custom-call(bf16[208,1536]{1,0:T(8,128)(2,1)} %bitcast.5, f32[3,1536]{1,0:T(4,128)} %mod.1, f32[2,1536]{1,0:T(2,128)} %cn.1, f32[4,768]{1,0:T(4,128)} %ng.1, bf16[48,4608]{1,0:T(8,128)(2,1)} %w_in.1, bf16[512,1536]{1,0:T(8,128)(2,1)} %ts_in.1, bf16[48,1536]{1,0:T(8,128)(2,1)} %bitcast.6, ...), custom_call_target="tpu_custom_call" | custom-call | flops 6000000000 | bytes 6000000 | tf_op jit(solution)/shard_map/pallas_call | solution.py:519
  106.8 2.0 %copy.11 = bf16[1,2,104,1536]{3,2,1,0:T(8,128)(2,1)} copy(bf16[1,2,104,1536]{3,2,1,0:T(8,128)(2,1)} %bitcast.4) | data formatting | bytes 1277952
